TPU v7x, 512 devices: a whole 4x4x16 slice. The times are simulated.
512 devices in a mesh: group: 16 (over y, x), dev: 32 (over z, core).
Axes of the slice: x: 4, y: 4, z: 16, core: 2. Of those that a mesh axis runs over, the one named last changes fastest.
Arguments:
- cam_jac: float32 [18, 2162688], P(None, ('group', 'dev')), may hold values from -1 to 1
- point_jac: float32 [6, 2162688], P(None, ('group', 'dev')), may hold values from -3 to 3
- residuals: float32 [2, 2162688], P(None, ('group', 'dev')), may hold values from -15 to 15
- obs_camera: int32 [2162688], P(('group', 'dev')), may hold values from 0 to 127
- obs_point: int32 [2162688], P(('group', 'dev')), may hold values from 0 to 1023
- obs_count: int32 [512, 33], P(('group', 'dev')), may hold values from 42 to 128, as said below
- cam_damp: float32 [9, 65536], P(None, ('group', 'dev')), may hold values from 0.3 to 3
- pt_damp: float32 [3, 524288], P(None, ('group', 'dev')), may hold values from 0.3 to 3
- partner_mask: int32 [32], P('dev'), may hold values from 1 to 15
Outputs:
- update: float32 [9, 65536], P(None, ('group', 'dev'))
- remainder: float32 [9, 65536], P(None, ('group', 'dev'))
Inputs may be any that keep to these rules, and one draw needn't show every extreme that they name: `obs_count`: slots at or beyond a count are padding. Every device's row holds one count equal to 128. For each index d within a partition, partitions g and g XOR partner_mask[d] are matched.
All inputs are finite; a program needn't handle non-finite values.
Results may differ from a plain program's by a relative error of at most 0.0085.
Values sent between devices are 32-bit elements; how exact they have to be, the bound alone decides.
No kernel may reach another device: no remote copies, remote signals or barrier semaphores. Data moves between devices by JAX's collectives and lax.ppermute only.
A program may use at most 64 MiB of HBM per device.

v0:
```python
import jax
import jax.numpy as jnp
from jax import lax
from jax.sharding import PartitionSpec as P

ITERS = 2


def partner_2(block, axis, distance):
    count = lax.axis_size(axis)
    route = []
    for low in range(count):
        high = low | 1 << distance
        if high != low and high < count:
            route += [(low, high), (high, low)]
    return lax.ppermute(block, axis, route)


def seg_rows(entries, indices, item_count):
    return jax.vmap(lambda single: jax.ops.segment_sum(single, indices, num_segments=item_count))(
        entries
    )


def cam_apply(cam_rows, cam_values):
    first_row = jnp.sum(cam_rows[0:9] * cam_values, axis=0)
    second_row = jnp.sum(cam_rows[9:18] * cam_values, axis=0)
    return jnp.stack([first_row, second_row])


def cam_spread(cam_rows, slot_values):
    return cam_rows[0:9] * slot_values[0:1] + cam_rows[9:18] * slot_values[1:2]


def point_apply(point_rows, point_values):
    first_row = jnp.sum(point_rows[0:3] * point_values, axis=0)
    second_row = jnp.sum(point_rows[3:6] * point_values, axis=0)
    return jnp.stack([first_row, second_row])


def point_spread(point_rows, slot_values):
    return point_rows[0:3] * slot_values[0:1] + point_rows[3:6] * slot_values[1:2]


def point_blocks(point_rows, point_ids, damping):
    item_count = damping.shape[1]
    summands = []
    for first_axis, second_axis in ((0, 0), (0, 1), (0, 2), (1, 1), (1, 2), (2, 2)):
        summands.append(
            point_rows[first_axis] * point_rows[second_axis]
            + point_rows[3 + first_axis] * point_rows[3 + second_axis]
        )
    blocks = seg_rows(jnp.stack(summands), point_ids, item_count)
    nothing = jnp.zeros_like(damping[0])
    return blocks + jnp.stack([damping[0], nothing, nothing, damping[1], nothing, damping[2]])


def solve_three(blocks, source):
    cofactor_xx = blocks[3] * blocks[5] - blocks[4] * blocks[4]
    cofactor_xy = blocks[2] * blocks[4] - blocks[1] * blocks[5]
    cofactor_xz = blocks[1] * blocks[4] - blocks[2] * blocks[3]
    cofactor_yy = blocks[0] * blocks[5] - blocks[2] * blocks[2]
    cofactor_yz = blocks[1] * blocks[2] - blocks[0] * blocks[4]
    cofactor_zz = blocks[0] * blocks[3] - blocks[1] * blocks[1]
    determinant = blocks[0] * cofactor_xx + blocks[1] * cofactor_xy + blocks[2] * cofactor_xz
    first_out = cofactor_xx * source[0] + cofactor_xy * source[1] + cofactor_xz * source[2]
    second_out = cofactor_xy * source[0] + cofactor_yy * source[1] + cofactor_yz * source[2]
    third_out = cofactor_xz * source[0] + cofactor_yz * source[1] + cofactor_zz * source[2]
    return jnp.stack([first_out, second_out, third_out]) / determinant


def across(values, partner, swapper, bit_count):
    for bit_index in range(bit_count):
        moved = swapper(values, bit_index)
        chosen = jnp.bitwise_and(jnp.right_shift(partner, bit_index), 1) == 1
        values = jnp.where(chosen, moved, values)
    return values


def on_device(
    cam_jac, point_jac, residuals, obs_camera, obs_point, obs_count, cam_damp, pt_damp, partner_mask
):
    members = lax.axis_size("dev")
    bit_count = lax.axis_size("group").bit_length() - 1
    block_count = members + 1
    slot_total = cam_jac.shape[1]
    slot_size = slot_total // block_count
    inner_total = members * slot_size
    cam_count = cam_damp.shape[1]
    point_count = pt_damp.shape[1]
    partner = partner_mask[0]
    live = (
        (jnp.arange(slot_size, dtype=jnp.int32)[None, :] < obs_count[0][:, None])
        .reshape(-1)
        .astype(jnp.float32)
    )
    cam_rows = cam_jac * live
    point_rows = point_jac * live
    blocks = point_blocks(point_rows, obs_point, pt_damp)

    def point_side(moved):
        pulled = solve_three(
            blocks, seg_rows(point_spread(point_rows, moved), obs_point, point_count)
        )
        return moved - point_apply(point_rows, pulled[:, obs_point])

    reduced = point_side(residuals)
    payload = jnp.concatenate([cam_rows, reduced, obs_camera.astype(jnp.float32)[None, :]], 0)
    arrived_inner = lax.all_to_all(
        payload[:, :inner_total], "dev", split_axis=1, concat_axis=1, tiled=True
    )
    arrived_outer = across(
        payload[:, inner_total:],
        partner,
        lambda values, bit_index: partner_2(values, "group", bit_index),
        bit_count,
    )
    arrived = jnp.concatenate([arrived_inner, arrived_outer], 1)
    owned_rows = arrived[0:18]
    owned_ids = arrived[20].astype(jnp.int32)
    gradient = -seg_rows(cam_spread(owned_rows, arrived[18:20]), owned_ids, cam_count)
    diagonal = cam_damp + seg_rows(
        owned_rows[0:9] ** 2 + owned_rows[9:18] ** 2, owned_ids, cam_count
    )

    def schur(direction):
        moved = cam_apply(owned_rows, direction[:, owned_ids])
        sent_inner = lax.all_to_all(
            moved[:, :inner_total], "dev", split_axis=1, concat_axis=1, tiled=True
        )
        sent_outer = across(
            moved[:, inner_total:],
            partner,
            lambda values, bit_index: partner_2(values, "group", bit_index),
            bit_count,
        )
        kept = point_side(jnp.concatenate([sent_inner, sent_outer], 1))
        back_inner = lax.all_to_all(
            kept[:, :inner_total], "dev", split_axis=1, concat_axis=1, tiled=True
        )
        back_outer = across(
            kept[:, inner_total:],
            partner,
            lambda values, bit_index: partner_2(values, "group", bit_index),
            bit_count,
        )
        returned = jnp.concatenate([back_inner, back_outer], 1)
        return cam_damp * direction + seg_rows(
            cam_spread(owned_rows, returned), owned_ids, cam_count
        )

    precond = 1.0 / diagonal
    update = jnp.zeros_like(gradient)
    remainder = gradient
    scaled = precond * remainder
    direction = scaled
    norm_now = lax.psum(jnp.sum(remainder * scaled), ("group", "dev"))
    for step_index in range(ITERS):
        image = schur(direction)
        curvature = lax.psum(jnp.sum(direction * image), ("group", "dev"))
        step_size = norm_now / curvature
        update = update + step_size * direction
        remainder = remainder - step_size * image
        if step_index + 1 < ITERS:
            scaled = precond * remainder
            norm_next = lax.psum(jnp.sum(remainder * scaled), ("group", "dev"))
            direction = scaled + norm_next / norm_now * direction
            norm_now = norm_next
    return (update, remainder)


def solution(mesh):
    return jax.shard_map(
        on_device,
        mesh=mesh,
        in_specs=(
            P(None, ("group", "dev")),
            P(None, ("group", "dev")),
            P(None, ("group", "dev")),
            P(("group", "dev")),
            P(("group", "dev")),
            P(("group", "dev"), None),
            P(None, ("group", "dev")),
            P(None, ("group", "dev")),
            P("dev"),
        ),
        out_specs=(P(None, ("group", "dev")), P(None, ("group", "dev"))),
        check_vma=False,
    )
```

profile of v0, /device:TPU:1, one launch (start us, length us, event | category | flops | bytes accessed | tf_op | source)
XLA Modules:
  0.0 864.4 jit_solution(16352821904402981239)
XLA Ops:
  1.4 2.9 copy.240
  4.3 3.0 broadcast_multiply_fusion
  7.3 7.5 fusion.96
  31.1 25.9 %scatter_fusion = f32[6,1024]{0,1:T(8,128)S(1)} fusion(f32[6,1024]{0,1:T(8,128)S(1)} %copy.265, s32[4224]{0:T(1024)S(1)} %copy-done.11, f32[4224,6]{1,0:T(8,128)} %copy.266), kind=kCustom, calls=%fused_computation.5 | custom fusion | flops 25344 | bytes 321024 | tf_op jit(solution)/shard_map/vmap()/scatter-add | solution.py:20
  64.6 28.7 %scatter_custom_fusion.1 = f32[3,1024]{0,1:T(8,128)S(1)} fusion(s32[4224]{0:T(1024)S(1)} %copy-done.11, f32[6,4224]{0,1:T(8,128)S(1)} %broadcast_multiply_fusion, f32[4224]{0:T(1024)S(1)} %get-tuple-element.37, f32[4224]{0:T(1024)S(1)} %get-tuple-element.36, f32[]{:T(128)} %constant.12.clone.1), kind=kCustom, calls=%fused_computation.45 | custom fusion | flops 50688 | bytes 4378628 | tf_op jit(solution)/shard_map/vmap()/scatter-add | solution.py:20
  98.9 8.7 %gather_fusion = f32[4224,3]{1,0:T(8,128)} fusion(f32[3,1024]{0,1:T(8,128)S(1)} %copy.276, s32[5120]{0:T(1024)S(1)} %pad_clamp_fusion.1), kind=kCustom, calls=%fused_computation | custom fusion | bytes 118272 | tf_op jit(solution)/shard_map/gather | solution.py:105
  107.6 3.4 fusion.21
  112.4 16.7 %all-to-all-start = ((f32[21,32,128]{2,0,1:T(8,128)}), f32[21,32,128]{2,0,1:T(8,128)S(1)}, u32[]{:S(2)}, u32[]{:S(2)}) async-start(f32[21,32,128]{2,0,1:T(8,128)} %copy.277), calls=%async_computation | async-start | bytes 786432 | tf_op jit(solution)/shard_map/all_to_all | solution.py:109
  129.1 3.1 collective-permute-start
  133.6 4.6 collective-permute-start.1
  139.8 3.2 collective-permute-start.2
  144.5 4.8 collective-permute-start.3
  150.5 6.6 all-to-all-done
  161.9 26.1 %scatter_custom_fusion.3 = f32[9,128]{0,1:T(8,128)S(1)} fusion(f32[9,128]{0,1:T(8,128)S(1)} %copy.314, s32[4224]{0:T(1024)S(1)} %reduce.2, f32[9,4224]{0,1:T(8,128)} %copy.304, f32[9,4224]{0,1:T(8,128)} %copy.303), kind=kCustom, calls=%fused_computation.37 | custom fusion | flops 152064 | bytes 308736 | tf_op jit(solution)/shard_map/vmap()/scatter-add | solution.py:20
  188.0 28.5 %scatter_custom_fusion.2 = f32[9,128]{0,1:T(8,128)S(1)} fusion(s32[4224]{0:T(1024)S(1)} %reduce.2, f32[9,4224]{0,1:T(8,128)} %copy.304, f32[9,4224]{0,1:T(8,128)} %copy.303, f32[4224]{0:T(1024)S(1)} %get-tuple-element.25, f32[4224]{0:T(1024)S(1)} %get-tuple-element.24, f32[]{:T(128)} %constant.12.clone.1), kind=kCustom, calls=%fused_computation.39 | custom fusion | flops 152064 | bytes 349700 | tf_op jit(solution)/shard_map/vmap()/scatter-add | solution.py:20
  216.6 8.7 %gather_fusion.1 = f32[4224,9]{1,0:T(8,128)} fusion(f32[9,128]{0,1:T(8,128)S(1)} %get-tuple-element.47, s32[5120]{0:T(1024)S(1)} %pad_clamp_fusion), kind=kCustom, calls=%fused_computation.1 | custom fusion | bytes 321024 | tf_op jit(solution)/shard_map/gather | solution.py:127
  225.3 4.1 fusion.15
  229.5 3.1 collective-permute-start.4
  233.8 4.7 collective-permute-start.5
  239.6 3.2 collective-permute-start.6
  243.9 4.8 collective-permute-start.7
  249.4 13.3 %all-to-all-start.1 = ((f32[2,32,128]{2,0,1:T(2,128)}), f32[2,32,128]{2,0,1:T(2,128)S(1)}, u32[]{:S(2)}, u32[]{:S(2)}) async-start(f32[2,32,128]{2,0,1:T(2,128)} %fusion.73), calls=%async_computation.1 | async-start | bytes 65536 | tf_op jit(solution)/shard_map/all_to_all | solution.py:128
  262.7 12.1 %all-to-all-done.1 = f32[2,32,128]{2,0,1:T(2,128)S(1)} async-done(((f32[2,32,128]{2,0,1:T(2,128)}), f32[2,32,128]{2,0,1:T(2,128)S(1)}, u32[]{:S(2)}, u32[]{:S(2)}) %all-to-all-start.1) | async-done | bytes 32800 | tf_op jit(solution)/shard_map/all_to_all | solution.py:128
  275.4 28.8 %scatter_custom_fusion.4 = f32[3,1024]{0,1:T(8,128)S(1)} fusion(s32[4224]{0:T(1024)} %param.13, f32[6,4224]{0,1:T(8,128)S(1)} %broadcast_multiply_fusion, f32[4224]{0:T(1024)S(1)} %get-tuple-element.35, f32[4224]{0:T(1024)S(1)} %get-tuple-element.34, f32[]{:T(128)} %constant.12.clone.1), kind=kCustom, calls=%fused_computation.31 | custom fusion | flops 50688 | bytes 4379136 | tf_op jit(solution)/shard_map/vmap()/scatter-add | solution.py:20
  309.8 9.5 %gather_fusion.2 = f32[4224,3]{1,0:T(8,128)} fusion(f32[3,1024]{0,1:T(8,128)S(1)} %copy.286, s32[5120]{0:T(1024)} %copy-done.4), kind=kCustom, calls=%fused_computation.2 | custom fusion | bytes 118272 | tf_op jit(solution)/shard_map/gather | solution.py:105
  319.3 3.4 fusion.11
  322.8 3.1 collective-permute-start.8
  327.1 4.6 collective-permute-start.9
  340.3 8.0 all-to-all-start.2
  348.3 12.3 %all-to-all-done.2 = f32[2,32,128]{2,0,1:T(2,128)S(1)} async-done(((f32[2,32,128]{2,0,1:T(2,128)}), f32[2,32,128]{2,0,1:T(2,128)S(1)}, u32[]{:S(2)}, u32[]{:S(2)}) %all-to-all-start.2) | async-done | bytes 32800 | tf_op jit(solution)/shard_map/all_to_all | solution.py:138
  360.7 29.0 %scatter_custom_fusion.5 = f32[9,128]{0,1:T(8,128)S(1)} fusion(f32[9,128]{0,1:T(8,128)S(1)} %get-tuple-element.46, s32[4224]{0:T(1024)} %copy-done.17, f32[9,4224]{0,1:T(8,128)} %copy.304, f32[9,4224]{0,1:T(8,128)} %copy.303, f32[4224]{0:T(1024)S(1)} %get-tuple-element.33, f32[4224]{0:T(1024)S(1)} %get-tuple-element.32), kind=kCustom, calls=%fused_computation.25 | custom fusion | flops 152064 | bytes 4370944 | tf_op jit(solution)/shard_map/vmap()/scatter-add | solution.py:20
  390.3 101.9 %all-reduce = (f32[]{:T(128)}, f32[]{:T(128)}) all-reduce(f32[]{:T(128)} %get-tuple-element.27, f32[]{:T(128)} %get-tuple-element.26), channel_id=1, replica_groups=mesh['group'=16,'dev'=32] {'group','dev'}, use_global_device_ids=true, to_apply=%region_7.8 | all-reduce | flops 2 | bytes 16 | tf_op jit(solution)/shard_map/psum | solution.py:157
  494.1 99.5 %psum.30 = f32[]{:T(128)} all-reduce(f32[]{:T(128)} %get-tuple-element.42), channel_id=1, replica_groups=mesh['group'=16,'dev'=32] {'group','dev'}, use_global_device_ids=true, to_apply=%region_17.18 | all-reduce | flops 1 | bytes 8 | tf_op jit(solution)/shard_map/psum | solution.py:166
  595.0 8.7 %gather_fusion.3 = f32[4224,9]{1,0:T(8,128)} fusion(f32[9,128]{0,1:T(8,128)S(1)} %get-tuple-element.41, s32[5120]{0:T(1024)S(1)} %copy-done.9), kind=kCustom, calls=%fused_computation.3 | custom fusion | bytes 321024 | tf_op jit(solution)/shard_map/gather | solution.py:127
  603.7 4.1 fusion.7
  612.2 3.1 collective-permute-start.13
  622.4 3.2 collective-permute-start.15
  626.2 10.0 %all-to-all-start.3 = ((f32[2,32,128]{2,0,1:T(2,128)}), f32[2,32,128]{2,0,1:T(2,128)S(1)}, u32[]{:S(2)}, u32[]{:S(2)}) async-start(f32[2,32,128]{2,0,1:T(2,128)} %fusion.71), calls=%async_computation.3 | async-start | bytes 65536 | tf_op jit(solution)/shard_map/all_to_all | solution.py:128
  636.2 12.1 %all-to-all-done.3 = f32[2,32,128]{2,0,1:T(2,128)S(1)} async-done(((f32[2,32,128]{2,0,1:T(2,128)}), f32[2,32,128]{2,0,1:T(2,128)S(1)}, u32[]{:S(2)}, u32[]{:S(2)}) %all-to-all-start.3) | async-done | bytes 32800 | tf_op jit(solution)/shard_map/all_to_all | solution.py:128
  648.4 29.0 %scatter_custom_fusion.6 = f32[3,1024]{0,1:T(8,128)S(1)} fusion(s32[4224]{0:T(1024)} %param.13, f32[6,4224]{0,1:T(8,128)S(1)} %broadcast_multiply_fusion, f32[4224]{0:T(1024)S(1)} %get-tuple-element.31, f32[4224]{0:T(1024)S(1)} %get-tuple-element.30, f32[]{:T(128)} %constant.12.clone.1), kind=kCustom, calls=%fused_computation.19 | custom fusion | flops 50688 | bytes 4379136 | tf_op jit(solution)/shard_map/vmap()/scatter-add | solution.py:20
  681.7 8.7 %gather_fusion.4 = f32[4224,3]{1,0:T(8,128)} fusion(f32[3,1024]{0,1:T(8,128)S(1)} %copy.291, s32[5120]{0:T(1024)S(1)} %copy-done.5), kind=kCustom, calls=%fused_computation.4 | custom fusion | bytes 118272 | tf_op jit(solution)/shard_map/gather | solution.py:105
  690.4 3.4 fusion.3
  701.0 3.1 collective-permute-done.17
  708.4 3.6 collective-permute-start.19
  712.5 8.3 all-to-all-start.4
  720.9 12.3 %all-to-all-done.4 = f32[2,32,128]{2,0,1:T(2,128)S(1)} async-done(((f32[2,32,128]{2,0,1:T(2,128)}), f32[2,32,128]{2,0,1:T(2,128)S(1)}, u32[]{:S(2)}, u32[]{:S(2)}) %all-to-all-start.4) | async-done | bytes 32800 | tf_op jit(solution)/shard_map/all_to_all | solution.py:138
  733.2 28.6 %scatter_custom_fusion.7 = f32[9,128]{0,1:T(8,128)S(1)} fusion(f32[9,128]{0,1:T(8,128)S(1)} %get-tuple-element.40, s32[4224]{0:T(1024)} %copy-done.17, f32[9,4224]{0,1:T(8,128)} %copy.304, f32[9,4224]{0,1:T(8,128)} %copy.303, f32[4224]{0:T(1024)S(1)} %get-tuple-element.29, f32[4224]{0:T(1024)S(1)} %get-tuple-element.28), kind=kCustom, calls=%fused_computation.13 | custom fusion | flops 152064 | bytes 4370944 | tf_op jit(solution)/shard_map/vmap()/scatter-add | solution.py:20
  762.5 99.0 %psum.31 = f32[]{:T(128)} all-reduce(f32[]{:T(128)} %multiply_reduce_fusion), channel_id=1, replica_groups=mesh['group'=16,'dev'=32] {'group','dev'}, use_global_device_ids=true, to_apply=%region_25.26 | all-reduce | flops 1 | bytes 8 | tf_op jit(solution)/shard_map/psum | solution.py:160
  (192 shorter events, 92.8 us)
Async XLA Ops:
  26.1 4.6 copy-start.20
  28.4 2.7 copy-start.11
  59.1 5.0 copy-start
  59.1 5.4 copy-start.10
  97.3 1.3 copy-start.12
  98.8 12.2 %copy-start.4 = (s32[5120]{0:T(1024)}, s32[5120]{0:T(1024)S(1)}, u32[]{:S(2)}) copy-start(s32[5120]{0:T(1024)S(1)} %pad_clamp_fusion.1) | copy-start | bytes 61444
  107.6 3.5 copy-start.3
  107.6 3.5 copy-start.16
  111.3 38.1 %copy-start.21 = (f32[9,128]{1,0:T(8,128)S(1)}, f32[9,128]{1,0:T(8,128)}, u32[]{:S(2)}) copy-start(f32[9,128]{1,0:T(8,128)} %param.15) | copy-start | bytes 13828
  112.4 44.7 %all-to-all-start = ((f32[21,32,128]{2,0,1:T(8,128)}), f32[21,32,128]{2,0,1:T(8,128)S(1)}, u32[]{:S(2)}, u32[]{:S(2)}) async-start(f32[21,32,128]{2,0,1:T(8,128)} %copy.277), calls=%async_computation | async-start | bytes 786432 | tf_op jit(solution)/shard_map/all_to_all | solution.py:109
  129.1 4.4 collective-permute-start
  133.6 6.2 collective-permute-start.1
  139.8 4.7 collective-permute-start.2
  144.5 5.9 collective-permute-start.3
  161.8 54.8 %copy-start.8 = (s32[5120]{0:T(1024)}, s32[5120]{0:T(1024)S(1)}, u32[]{:S(2)}) copy-start(s32[5120]{0:T(1024)S(1)} %pad_clamp_fusion) | copy-start | bytes 61444
  161.8 26.1 %copy-start.17 = (s32[4224]{0:T(1024)}, s32[4224]{0:T(1024)S(1)}, u32[]{:S(2)}) copy-start(s32[4224]{0:T(1024)S(1)} %reduce.2) | copy-start | bytes 50692
  229.5 4.3 collective-permute-start.4
  233.8 5.8 collective-permute-start.5
  239.6 4.3 collective-permute-start.6
  243.9 18.8 %collective-permute-start.7 = (f32[2,128]{1,0:T(2,128)S(1)}, f32[2,128]{1,0:T(2,128)S(1)}, u32[]{:S(2)}, u32[]{:S(2)}) collective-permute-start(f32[2,128]{1,0:T(2,128)S(1)} %broadcast_select_fusion.15), channel_id=1, source_target_pairs={{0,256},{256,0},{32,288},{288,32},{64,320},{320,64},{96,352},{352,... | collective-permute-start | bytes 3080 | tf_op jit(solution)/shard_map/ppermute | solution.py:16
  249.4 25.4 %all-to-all-start.1 = ((f32[2,32,128]{2,0,1:T(2,128)}), f32[2,32,128]{2,0,1:T(2,128)S(1)}, u32[]{:S(2)}, u32[]{:S(2)}) async-start(f32[2,32,128]{2,0,1:T(2,128)} %fusion.73), calls=%async_computation.1 | async-start | bytes 65536 | tf_op jit(solution)/shard_map/all_to_all | solution.py:128
  262.7 12.7 %copy-start.18 = (f32[2,128]{1,0:T(2,128)}, f32[2,128]{1,0:T(2,128)S(1)}, u32[]{:S(2)}) copy-start(f32[2,128]{1,0:T(2,128)S(1)} %broadcast_select_fusion.19) | copy-start | bytes 3076
  274.8 0.6 copy-start.6
  319.3 3.4 copy-start.7
  319.3 3.4 copy-start.19
  322.8 4.3 collective-permute-start.8
  327.1 5.8 collective-permute-start.9
  332.9 4.3 collective-permute-start.10
  337.2 11.1 %collective-permute-start.11 = (f32[2,128]{1,0:T(2,128)S(1)}, f32[2,128]{1,0:T(2,128)S(1)}, u32[]{:S(2)}, u32[]{:S(2)}) collective-permute-start(f32[2,128]{1,0:T(2,128)S(1)} %broadcast_select_fusion.14), channel_id=1, source_target_pairs={{0,256},{256,0},{32,288},{288,32},{64,320},{320,64},{96,352},{352,... | collective-permute-start | bytes 3080 | tf_op jit(solution)/shard_map/ppermute | solution.py:16
  340.3 20.3 %all-to-all-start.2 = ((f32[2,32,128]{2,0,1:T(2,128)}), f32[2,32,128]{2,0,1:T(2,128)S(1)}, u32[]{:S(2)}, u32[]{:S(2)}) async-start(f32[2,32,128]{2,0,1:T(2,128)} %slice_bitcast_fusion.1), calls=%async_computation.2 | async-start | bytes 65536 | tf_op jit(solution)/shard_map/all_to_all | solution.py:138
  360.7 234.3 %copy-start.9 = (s32[5120]{0:T(1024)S(1)}, s32[5120]{0:T(1024)}, u32[]{:S(2)}) copy-start(s32[5120]{0:T(1024)} %copy-done.8) | copy-start | bytes 61444
  494.1 113.7 %copy-start.1 = (f32[9,128]{0,1:T(8,128)}, f32[9,128]{0,1:T(8,128)S(1)}, u32[]{:S(2)}) copy-start(f32[9,128]{0,1:T(8,128)S(1)} %get-tuple-element.43) | copy-start | bytes 13828
  607.9 4.3 collective-permute-start.12
  612.2 5.8 collective-permute-start.13
  618.1 4.3 collective-permute-start.14
  622.4 13.8 %collective-permute-start.15 = (f32[2,128]{1,0:T(2,128)S(1)}, f32[2,128]{1,0:T(2,128)S(1)}, u32[]{:S(2)}, u32[]{:S(2)}) collective-permute-start(f32[2,128]{1,0:T(2,128)S(1)} %broadcast_select_fusion.13), channel_id=1, source_target_pairs={{0,256},{256,0},{32,288},{288,32},{64,320},{320,64},{96,352},{352,... | collective-permute-start | bytes 3080 | tf_op jit(solution)/shard_map/ppermute | solution.py:16
  626.2 22.1 %all-to-all-start.3 = ((f32[2,32,128]{2,0,1:T(2,128)}), f32[2,32,128]{2,0,1:T(2,128)S(1)}, u32[]{:S(2)}, u32[]{:S(2)}) async-start(f32[2,32,128]{2,0,1:T(2,128)} %fusion.71), calls=%async_computation.3 | async-start | bytes 65536 | tf_op jit(solution)/shard_map/all_to_all | solution.py:128
  677.4 3.9 copy-start.14
  677.5 3.9 copy-start.15
  677.5 4.0 copy-start.13
  677.5 4.2 copy-start.5
  693.9 4.3 collective-permute-start.16
  698.2 5.8 collective-permute-start.17
  704.1 4.3 collective-permute-start.18
  708.4 12.5 %collective-permute-start.19 = (f32[2,128]{1,0:T(2,128)S(1)}, f32[2,128]{1,0:T(2,128)S(1)}, u32[]{:S(2)}, u32[]{:S(2)}) collective-permute-start(f32[2,128]{1,0:T(2,128)S(1)} %broadcast_select_fusion.12), channel_id=1, source_target_pairs={{0,256},{256,0},{32,288},{288,32},{64,320},{320,64},{96,352},{352,... | collective-permute-start | bytes 3080 | tf_op jit(solution)/shard_map/ppermute | solution.py:16
  712.5 20.6 %all-to-all-start.4 = ((f32[2,32,128]{2,0,1:T(2,128)}), f32[2,32,128]{2,0,1:T(2,128)S(1)}, u32[]{:S(2)}, u32[]{:S(2)}) async-start(f32[2,32,128]{2,0,1:T(2,128)} %slice_bitcast_fusion), calls=%async_computation.4 | async-start | bytes 65536 | tf_op jit(solution)/shard_map/all_to_all | solution.py:138
  733.2 129.6 %copy-start.2 = (f32[9,128]{0,1:T(8,128)S(1)}, f32[9,128]{0,1:T(8,128)}, u32[]{:S(2)}) copy-start(f32[9,128]{0,1:T(8,128)} %copy-done.1) | copy-start | bytes 13828
where the time goes:
time: 873 us; the launch traced here: 864 us
  blocking collectives  300 us (34%)
  other arithmetic  254 us (29%)
  starting transfers between devices  122 us (14%)
  local copies, waits for them, and re-layouts  99.9 us (11%)
  waiting for transfers between devices  81.4 us (9%)
    scatter-add x8, other arithmetic, seg_rows(): jax.ops.segment_sum(single, indices, num_segments=item_count)  225 us
    psum x1, blocking collectives, on_device(): norm_now = lax.psum(jnp.sum(remainder * scaled), ('group', 'dev'))  102 us
    psum x1, blocking collectives, on_device(): norm_next = lax.psum(jnp.sum(remainder * scaled), ('group', 'dev'))  99.5 us
    psum x1, blocking collectives, on_device(): curvature = lax.psum(jnp.sum(direction * image), ('group', 'dev'))  99 us
    ppermute x20, starting transfers between devices, partner_2(): return lax.ppermute(block, axis, route)  66 us
    gather x3, local copies, waits for them, and re-layouts, point_side(): return moved - point_apply(point_rows, pulled[:, obs_point])  26.9 us
    ppermute x20, waiting for transfers between devices, partner_2(): return lax.ppermute(block, axis, route)  26.1 us
    all_to_all x2, waiting for transfers between devices, schur(): lax.all_to_all(kept[:, :inner_total], 'dev', split_axis=1, concat_axis=1,...  24.5 us
  transfers between devices with their start and end apart: 25, of which 21 were waited for; matrix products, arithmetic and copies ran while one was open for 0% of the time, Pallas kernels for 0%

commit v1 on v0

--- a/solution.py
+++ b/solution.py
@@ -135,8 +135,14 @@
             bit_count,
         )
         kept = point_side(jnp.concatenate([sent_inner, sent_outer], 1))
-        back_inner = lax.all_to_all(
-            kept[:, :inner_total], "dev", split_axis=1, concat_axis=1, tiled=True
+        back_inner = jnp.concatenate(
+            lax.all_to_all(
+                jnp.stack(jnp.split(kept[:, :inner_total], lax.axis_size("dev"), axis=1)),
+                "dev",
+                0,
+                0,
+            ),
+            axis=1,
         )
         back_outer = across(
             kept[:, inner_total:],

time: 873 us -> 905 us (1.037)
  local copies, waits for them, and re-layouts: 99.9 us -> 135 us
    unnamed x69 -> x131, local copies, waits for them, and re-layouts: 22.7 us -> 58.2 us
  transfers between devices with their start and end apart: 25 -> 25, of which waited for: 21 -> 21; matrix products, arithmetic and copies ran while one was open for 0% -> 1% of each run, Pallas kernels for 0% -> 0%
where the time goes in v1:
time: 905 us; the launch traced here: 896 us
  blocking collectives  300 us (33%)
  other arithmetic  254 us (28%)
  local copies, waits for them, and re-layouts  135 us (15%)
  starting transfers between devices  122 us (13%)
  waiting for transfers between devices  78 us (9%)
    scatter-add x8, other arithmetic, seg_rows(): jax.ops.segment_sum(single, indices, num_segments=item_count)  225 us
    psum x1, blocking collectives, on_device(): norm_now = lax.psum(jnp.sum(remainder * scaled), ('group', 'dev'))  102 us
    psum x1, blocking collectives, on_device(): norm_next = lax.psum(jnp.sum(remainder * scaled), ('group', 'dev'))  99.5 us
    psum x1, blocking collectives, on_device(): curvature = lax.psum(jnp.sum(direction * image), ('group', 'dev'))  99 us
    ppermute x20, starting transfers between devices, partner_2(): return lax.ppermute(block, axis, route)  65.9 us
    unnamed x131, local copies, waits for them, and re-layouts  58.2 us
    gather x3, local copies, waits for them, and re-layouts, point_side(): return moved - point_apply(point_rows, pulled[:, obs_point])  26.9 us
    all_to_all x2, waiting for transfers between devices, schur(): lax.all_to_all(jnp.stack(jnp.split(kept[:, :inner_total], lax.axis_size('...  24.5 us
  transfers between devices with their start and end apart: 25, of which 21 were waited for; matrix products, arithmetic and copies ran while one was open for 1% of the time, Pallas kernels for 0%

profile of v1, /device:TPU:1, one launch (start us, length us, event | category | flops | bytes accessed | tf_op | source)
XLA Modules:
  0.0 896.4 jit_solution(6077536501126430697)
XLA Ops:
  1.4 2.9 copy.240
  4.3 3.0 broadcast_multiply_fusion
  7.3 7.5 fusion.96
  31.1 25.9 %scatter_fusion = f32[6,1024]{0,1:T(8,128)S(1)} fusion(f32[6,1024]{0,1:T(8,128)S(1)} %copy.265, s32[4224]{0:T(1024)S(1)} %copy-done.11, f32[4224,6]{1,0:T(8,128)} %copy.266), kind=kCustom, calls=%fused_computation.5 | custom fusion | flops 25344 | bytes 321024 | tf_op jit(solution)/shard_map/vmap()/scatter-add | solution.py:20
  64.6 28.7 %scatter_custom_fusion.1 = f32[3,1024]{0,1:T(8,128)S(1)} fusion(s32[4224]{0:T(1024)S(1)} %copy-done.11, f32[6,4224]{0,1:T(8,128)S(1)} %broadcast_multiply_fusion, f32[4224]{0:T(1024)S(1)} %get-tuple-element.37, f32[4224]{0:T(1024)S(1)} %get-tuple-element.36, f32[]{:T(128)} %constant.12.clone.1), kind=kCustom, calls=%fused_computation.45 | custom fusion | flops 50688 | bytes 4378628 | tf_op jit(solution)/shard_map/vmap()/scatter-add | solution.py:20
  98.9 8.7 gather_fusion
  107.6 3.4 fusion.21
  112.4 16.7 %all-to-all-start = ((f32[21,32,128]{2,0,1:T(8,128)}), f32[21,32,128]{2,0,1:T(8,128)S(1)}, u32[]{:S(2)}, u32[]{:S(2)}) async-start(f32[21,32,128]{2,0,1:T(8,128)} %copy.277), calls=%async_computation | async-start | bytes 786432 | tf_op jit(solution)/shard_map/all_to_all | solution.py:109
  129.1 3.1 collective-permute-start
  133.6 4.6 collective-permute-start.1
  139.8 3.2 collective-permute-start.2
  144.5 4.8 collective-permute-start.3
  150.5 6.6 all-to-all-done
  161.9 26.1 %scatter_custom_fusion.3 = f32[9,128]{0,1:T(8,128)S(1)} fusion(f32[9,128]{0,1:T(8,128)S(1)} %copy.314, s32[4224]{0:T(1024)S(1)} %reduce.2, f32[9,4224]{0,1:T(8,128)} %copy.304, f32[9,4224]{0,1:T(8,128)} %copy.303), kind=kCustom, calls=%fused_computation.37 | custom fusion | flops 152064 | bytes 308736 | tf_op jit(solution)/shard_map/vmap()/scatter-add | solution.py:20
  188.0 28.5 %scatter_custom_fusion.2 = f32[9,128]{0,1:T(8,128)S(1)} fusion(s32[4224]{0:T(1024)S(1)} %reduce.2, f32[9,4224]{0,1:T(8,128)} %copy.304, f32[9,4224]{0,1:T(8,128)} %copy.303, f32[4224]{0:T(1024)S(1)} %get-tuple-element.25, f32[4224]{0:T(1024)S(1)} %get-tuple-element.24, f32[]{:T(128)} %constant.12.clone.1), kind=kCustom, calls=%fused_computation.39 | custom fusion | flops 152064 | bytes 349700 | tf_op jit(solution)/shard_map/vmap()/scatter-add | solution.py:20
  216.6 8.7 gather_fusion.1
  225.3 4.1 fusion.15
  229.5 3.1 collective-permute-start.4
  233.8 4.7 collective-permute-start.5
  239.6 3.2 collective-permute-start.6
  243.9 4.8 collective-permute-start.7
  249.4 13.3 %all-to-all-start.1 = ((f32[2,32,128]{2,0,1:T(2,128)}), f32[2,32,128]{2,0,1:T(2,128)S(1)}, u32[]{:S(2)}, u32[]{:S(2)}) async-start(f32[2,32,128]{2,0,1:T(2,128)} %fusion.73), calls=%async_computation.1 | async-start | bytes 65536 | tf_op jit(solution)/shard_map/all_to_all | solution.py:128
  262.7 12.1 %all-to-all-done.1 = f32[2,32,128]{2,0,1:T(2,128)S(1)} async-done(((f32[2,32,128]{2,0,1:T(2,128)}), f32[2,32,128]{2,0,1:T(2,128)S(1)}, u32[]{:S(2)}, u32[]{:S(2)}) %all-to-all-start.1) | async-done | bytes 32800 | tf_op jit(solution)/shard_map/all_to_all | solution.py:128
  275.4 28.8 %scatter_custom_fusion.4 = f32[3,1024]{0,1:T(8,128)S(1)} fusion(s32[4224]{0:T(1024)} %param.13, f32[6,4224]{0,1:T(8,128)S(1)} %broadcast_multiply_fusion, f32[4224]{0:T(1024)S(1)} %get-tuple-element.35, f32[4224]{0:T(1024)S(1)} %get-tuple-element.34, f32[]{:T(128)} %constant.12.clone.1), kind=kCustom, calls=%fused_computation.31 | custom fusion | flops 50688 | bytes 4379136 | tf_op jit(solution)/shard_map/vmap()/scatter-add | solution.py:20
  309.8 9.5 %gather_fusion.2 = f32[4224,3]{1,0:T(8,128)} fusion(f32[3,1024]{0,1:T(8,128)S(1)} %copy.286, s32[5120]{0:T(1024)} %copy-done.4), kind=kCustom, calls=%fused_computation.2 | custom fusion | bytes 118272 | tf_op jit(solution)/shard_map/gather | solution.py:105
  319.3 3.4 fusion.11
  338.8 3.1 collective-permute-start.8
  343.1 4.6 collective-permute-start.9
  356.3 8.0 all-to-all-start.2
  364.3 12.3 %all-to-all-done.2 = f32[32,2,128]{2,1,0:T(2,128)S(1)} async-done(((f32[32,2,128]{2,1,0:T(2,128)}), f32[32,2,128]{2,1,0:T(2,128)S(1)}, u32[]{:S(2)}, u32[]{:S(2)}) %all-to-all-start.2) | async-done | bytes 32800 | tf_op jit(solution)/shard_map/all_to_all | solution.py:139
  376.7 29.0 %scatter_custom_fusion.5 = f32[9,128]{0,1:T(8,128)S(1)} fusion(f32[9,128]{0,1:T(8,128)S(1)} %get-tuple-element.46, s32[4224]{0:T(1024)} %copy-done.17, f32[9,4224]{0,1:T(8,128)} %copy.304, f32[9,4224]{0,1:T(8,128)} %copy.303, f32[4224]{0:T(1024)S(1)} %get-tuple-element.33, f32[4224]{0:T(1024)S(1)} %get-tuple-element.32), kind=kCustom, calls=%fused_computation.25 | custom fusion | flops 152064 | bytes 4370944 | tf_op jit(solution)/shard_map/vmap()/scatter-add | solution.py:20
  406.3 101.9 %all-reduce = (f32[]{:T(128)}, f32[]{:T(128)}) all-reduce(f32[]{:T(128)} %get-tuple-element.27, f32[]{:T(128)} %get-tuple-element.26), channel_id=1, replica_groups=mesh['group'=16,'dev'=32] {'group','dev'}, use_global_device_ids=true, to_apply=%region_7.8 | all-reduce | flops 2 | bytes 16 | tf_op jit(solution)/shard_map/psum | solution.py:163
  510.1 99.5 %psum.30 = f32[]{:T(128)} all-reduce(f32[]{:T(128)} %get-tuple-element.42), channel_id=1, replica_groups=mesh['group'=16,'dev'=32] {'group','dev'}, use_global_device_ids=true, to_apply=%region_17.18 | all-reduce | flops 1 | bytes 8 | tf_op jit(solution)/shard_map/psum | solution.py:172
  611.0 8.7 gather_fusion.3
  619.7 4.1 fusion.7
  628.2 3.1 collective-permute-start.13
  638.4 3.2 collective-permute-start.15
  642.2 10.0 %all-to-all-start.3 = ((f32[2,32,128]{2,0,1:T(2,128)}), f32[2,32,128]{2,0,1:T(2,128)S(1)}, u32[]{:S(2)}, u32[]{:S(2)}) async-start(f32[2,32,128]{2,0,1:T(2,128)} %fusion.71), calls=%async_computation.3 | async-start | bytes 65536 | tf_op jit(solution)/shard_map/all_to_all | solution.py:128
  652.2 12.1 %all-to-all-done.3 = f32[2,32,128]{2,0,1:T(2,128)S(1)} async-done(((f32[2,32,128]{2,0,1:T(2,128)}), f32[2,32,128]{2,0,1:T(2,128)S(1)}, u32[]{:S(2)}, u32[]{:S(2)}) %all-to-all-start.3) | async-done | bytes 32800 | tf_op jit(solution)/shard_map/all_to_all | solution.py:128
  664.4 29.0 %scatter_custom_fusion.6 = f32[3,1024]{0,1:T(8,128)S(1)} fusion(s32[4224]{0:T(1024)} %param.13, f32[6,4224]{0,1:T(8,128)S(1)} %broadcast_multiply_fusion, f32[4224]{0:T(1024)S(1)} %get-tuple-element.31, f32[4224]{0:T(1024)S(1)} %get-tuple-element.30, f32[]{:T(128)} %constant.12.clone.1), kind=kCustom, calls=%fused_computation.19 | custom fusion | flops 50688 | bytes 4379136 | tf_op jit(solution)/shard_map/vmap()/scatter-add | solution.py:20
  697.7 8.7 gather_fusion.4
  706.4 3.4 fusion.3
  730.3 2.7 collective-permute-start.17
  740.4 3.6 collective-permute-start.19
  744.5 8.3 all-to-all-start.4
  752.9 12.3 %all-to-all-done.4 = f32[32,2,128]{2,1,0:T(2,128)S(1)} async-done(((f32[32,2,128]{2,1,0:T(2,128)}), f32[32,2,128]{2,1,0:T(2,128)S(1)}, u32[]{:S(2)}, u32[]{:S(2)}) %all-to-all-start.4) | async-done | bytes 32800 | tf_op jit(solution)/shard_map/all_to_all | solution.py:139
  765.2 28.6 %scatter_custom_fusion.7 = f32[9,128]{0,1:T(8,128)S(1)} fusion(f32[9,128]{0,1:T(8,128)S(1)} %get-tuple-element.40, s32[4224]{0:T(1024)} %copy-done.17, f32[9,4224]{0,1:T(8,128)} %copy.304, f32[9,4224]{0,1:T(8,128)} %copy.303, f32[4224]{0:T(1024)S(1)} %get-tuple-element.29, f32[4224]{0:T(1024)S(1)} %get-tuple-element.28), kind=kCustom, calls=%fused_computation.13 | custom fusion | flops 152064 | bytes 4370944 | tf_op jit(solution)/shard_map/vmap()/scatter-add | solution.py:20
  794.5 99.0 %psum.31 = f32[]{:T(128)} all-reduce(f32[]{:T(128)} %multiply_reduce_fusion), channel_id=1, replica_groups=mesh['group'=16,'dev'=32] {'group','dev'}, use_global_device_ids=true, to_apply=%region_25.26 | all-reduce | flops 1 | bytes 8 | tf_op jit(solution)/shard_map/psum | solution.py:166
  (254 shorter events, 125.1 us)
Async XLA Ops:
  26.1 4.6 copy-start.20
  28.4 2.7 copy-start.11
  59.1 5.0 copy-start
  59.1 5.4 copy-start.10
  97.3 1.3 copy-start.12
  98.8 12.2 %copy-start.4 = (s32[5120]{0:T(1024)}, s32[5120]{0:T(1024)S(1)}, u32[]{:S(2)}) copy-start(s32[5120]{0:T(1024)S(1)} %pad_clamp_fusion.1) | copy-start | bytes 61444
  107.6 3.5 copy-start.3
  107.6 3.5 copy-start.16
  111.3 38.1 %copy-start.21 = (f32[9,128]{1,0:T(8,128)S(1)}, f32[9,128]{1,0:T(8,128)}, u32[]{:S(2)}) copy-start(f32[9,128]{1,0:T(8,128)} %param.15) | copy-start | bytes 13828
  112.4 44.7 %all-to-all-start = ((f32[21,32,128]{2,0,1:T(8,128)}), f32[21,32,128]{2,0,1:T(8,128)S(1)}, u32[]{:S(2)}, u32[]{:S(2)}) async-start(f32[21,32,128]{2,0,1:T(8,128)} %copy.277), calls=%async_computation | async-start | bytes 786432 | tf_op jit(solution)/shard_map/all_to_all | solution.py:109
  129.1 4.4 collective-permute-start
  133.6 6.2 collective-permute-start.1
  139.8 4.7 collective-permute-start.2
  144.5 5.9 collective-permute-start.3
  161.8 54.8 %copy-start.8 = (s32[5120]{0:T(1024)}, s32[5120]{0:T(1024)S(1)}, u32[]{:S(2)}) copy-start(s32[5120]{0:T(1024)S(1)} %pad_clamp_fusion) | copy-start | bytes 61444
  161.8 26.1 %copy-start.17 = (s32[4224]{0:T(1024)}, s32[4224]{0:T(1024)S(1)}, u32[]{:S(2)}) copy-start(s32[4224]{0:T(1024)S(1)} %reduce.2) | copy-start | bytes 50692
  229.5 4.3 collective-permute-start.4
  233.8 5.8 collective-permute-start.5
  239.6 4.3 collective-permute-start.6
  243.9 18.8 %collective-permute-start.7 = (f32[2,128]{1,0:T(2,128)S(1)}, f32[2,128]{1,0:T(2,128)S(1)}, u32[]{:S(2)}, u32[]{:S(2)}) collective-permute-start(f32[2,128]{1,0:T(2,128)S(1)} %broadcast_select_fusion.15), channel_id=1, source_target_pairs={{0,256},{256,0},{32,288},{288,32},{64,320},{320,64},{96,352},{352,... | collective-permute-start | bytes 3080 | tf_op jit(solution)/shard_map/ppermute | solution.py:16
  249.4 25.4 %all-to-all-start.1 = ((f32[2,32,128]{2,0,1:T(2,128)}), f32[2,32,128]{2,0,1:T(2,128)S(1)}, u32[]{:S(2)}, u32[]{:S(2)}) async-start(f32[2,32,128]{2,0,1:T(2,128)} %fusion.73), calls=%async_computation.1 | async-start | bytes 65536 | tf_op jit(solution)/shard_map/all_to_all | solution.py:128
  262.7 12.7 %copy-start.18 = (f32[2,128]{1,0:T(2,128)}, f32[2,128]{1,0:T(2,128)S(1)}, u32[]{:S(2)}) copy-start(f32[2,128]{1,0:T(2,128)S(1)} %broadcast_select_fusion.19) | copy-start | bytes 3076
  274.8 0.6 copy-start.6
  319.3 3.4 copy-start.7
  319.3 3.4 copy-start.19
  338.8 4.3 collective-permute-start.8
  343.1 5.8 collective-permute-start.9
  349.0 4.3 collective-permute-start.10
  353.3 11.0 %collective-permute-start.11 = (f32[2,128]{1,0:T(2,128)S(1)}, f32[2,128]{1,0:T(2,128)S(1)}, u32[]{:S(2)}, u32[]{:S(2)}) collective-permute-start(f32[2,128]{1,0:T(2,128)S(1)} %broadcast_select_fusion.14), channel_id=1, source_target_pairs={{0,256},{256,0},{32,288},{288,32},{64,320},{320,64},{96,352},{352,... | collective-permute-start | bytes 3080 | tf_op jit(solution)/shard_map/ppermute | solution.py:16
  356.3 20.3 %all-to-all-start.2 = ((f32[32,2,128]{2,1,0:T(2,128)}), f32[32,2,128]{2,1,0:T(2,128)S(1)}, u32[]{:S(2)}, u32[]{:S(2)}) async-start(f32[32,2,128]{2,1,0:T(2,128)} %constant_dynamic-update-slice_fusion), calls=%async_computation.2 | async-start | bytes 65536 | tf_op jit(solution)/shard_map/all_to_all | solution.py:139
  376.7 234.3 %copy-start.9 = (s32[5120]{0:T(1024)S(1)}, s32[5120]{0:T(1024)}, u32[]{:S(2)}) copy-start(s32[5120]{0:T(1024)} %copy-done.8) | copy-start | bytes 61444
  510.1 113.7 %copy-start.1 = (f32[9,128]{0,1:T(8,128)}, f32[9,128]{0,1:T(8,128)S(1)}, u32[]{:S(2)}) copy-start(f32[9,128]{0,1:T(8,128)S(1)} %get-tuple-element.43) | copy-start | bytes 13828
  623.9 4.3 collective-permute-start.12
  628.2 5.8 collective-permute-start.13
  634.1 4.3 collective-permute-start.14
  638.4 13.8 %collective-permute-start.15 = (f32[2,128]{1,0:T(2,128)S(1)}, f32[2,128]{1,0:T(2,128)S(1)}, u32[]{:S(2)}, u32[]{:S(2)}) collective-permute-start(f32[2,128]{1,0:T(2,128)S(1)} %broadcast_select_fusion.13), channel_id=1, source_target_pairs={{0,256},{256,0},{32,288},{288,32},{64,320},{320,64},{96,352},{352,... | collective-permute-start | bytes 3080 | tf_op jit(solution)/shard_map/ppermute | solution.py:16
  642.2 22.1 %all-to-all-start.3 = ((f32[2,32,128]{2,0,1:T(2,128)}), f32[2,32,128]{2,0,1:T(2,128)S(1)}, u32[]{:S(2)}, u32[]{:S(2)}) async-start(f32[2,32,128]{2,0,1:T(2,128)} %fusion.71), calls=%async_computation.3 | async-start | bytes 65536 | tf_op jit(solution)/shard_map/all_to_all | solution.py:128
  693.4 3.9 copy-start.14
  693.5 3.9 copy-start.15
  693.5 4.0 copy-start.13
  693.5 4.2 copy-start.5
  726.0 4.3 collective-permute-start.16
  730.3 5.8 collective-permute-start.17
  736.1 4.3 collective-permute-start.18
  740.4 12.5 %collective-permute-start.19 = (f32[2,128]{1,0:T(2,128)S(1)}, f32[2,128]{1,0:T(2,128)S(1)}, u32[]{:S(2)}, u32[]{:S(2)}) collective-permute-start(f32[2,128]{1,0:T(2,128)S(1)} %broadcast_select_fusion.12), channel_id=1, source_target_pairs={{0,256},{256,0},{32,288},{288,32},{64,320},{320,64},{96,352},{352,... | collective-permute-start | bytes 3080 | tf_op jit(solution)/shard_map/ppermute | solution.py:16
  744.5 20.6 %all-to-all-start.4 = ((f32[32,2,128]{2,1,0:T(2,128)}), f32[32,2,128]{2,1,0:T(2,128)S(1)}, u32[]{:S(2)}, u32[]{:S(2)}) async-start(f32[32,2,128]{2,1,0:T(2,128)} %constant_dynamic-update-slice_fusion.32), calls=%async_computation.4 | async-start | bytes 65536 | tf_op jit(solution)/shard_map/all_to_all | solution.py:139
  765.2 129.6 %copy-start.2 = (f32[9,128]{0,1:T(8,128)S(1)}, f32[9,128]{0,1:T(8,128)}, u32[]{:S(2)}) copy-start(f32[9,128]{0,1:T(8,128)} %copy-done.1) | copy-start | bytes 13828
